TPU v7x, 1024 devices: a whole 8x8x8 slice. The times are simulated.
1024 devices in a mesh: replica: 64 (over z, x_lo, core), tensor: 16 (over y, x_hi).
Axes of the slice: x: 8 (x_hi: 2, x_lo: 4; x = x_hi * 4 + x_lo), y: 8, z: 8, core: 2. Of those that a mesh axis runs over, the one named last changes fastest.
Arguments:
- features: bfloat16 [81920, 5120], P('replica', 'tensor'), may hold values from -6 to 6
- key_grad: bfloat16 [81920, 512], P(('replica', 'tensor')), may hold values from -0.29882812 to 0.29882812
- master: float32 [64, 5120, 512], P('replica', 'tensor'), may hold values from -6 to 6
- exponents: int32 [2], replicated, may hold values from 0 to 5, as said below
Outputs:
- new_master: float32 [64, 5120, 512], P('replica', 'tensor')
- new_working: bfloat16 [64, 5120, 512], P('replica', 'tensor')
- input_grad: bfloat16 [81920, 5120], P('replica', 'tensor')
Inputs may be any that keep to these rules, and one draw needn't show every extreme that they name: Two different exponents: one of them is always 5 (the top bit of 64), the other lies in 0 to 4; either may come first.
All inputs are finite; a program needn't handle non-finite values.
Results may differ from a plain program's by a relative error of at most 0.006.
Values may be sent and summed in bfloat16 or wider, within the bound.
No kernel may reach another device: no remote copies, remote signals or barrier semaphores. Data moves between devices by JAX's collectives and lax.ppermute only.
A program may use at most 32 MiB of HBM per device.

v0:
```python
from functools import partial

import jax
import jax.numpy as jnp
from jax import lax
from jax.sharding import PartitionSpec as P

step_rate = 0.2


def from_partner(shard, axis, bit):
    return lax.ppermute(shard, axis, [(i, i ^ 1 << bit) for i in range(lax.axis_size(axis))])


def average_whole(values, hop_bit):
    arrived = from_partner(values, "replica", hop_bit)
    return 0.5 * (values + arrived)


def run_switch(which, helper, bit_count, values):
    return lax.switch(
        which, [partial(helper, hop_bit=hop_bit) for hop_bit in range(bit_count)], values
    )


def local(features, key_grad, master, exponents):
    shard = master[0]
    working = shard.astype(jnp.bfloat16)
    block_rows = lax.all_gather(key_grad, "tensor", axis=0, tiled=True)
    weight_grad = lax.dot_general(
        features, block_rows, (((0,), (0,)), ((), ())), preferred_element_type=jnp.float32
    )
    produced = lax.dot_general(
        block_rows, working, (((1,), (1,)), ((), ())), preferred_element_type=jnp.float32
    )
    input_rows = produced
    weight_grad, input_rows = (weight_grad, input_rows)
    stepped = shard - step_rate * weight_grad
    bit_count = lax.axis_size("replica").bit_length() - 1
    for which_round in range(2):
        stepped = run_switch(exponents[which_round], average_whole, bit_count, stepped)
    return (stepped[None], stepped.astype(jnp.bfloat16)[None], input_rows.astype(jnp.bfloat16))


def solution(mesh):
    in_specs = (
        P("replica", "tensor"),
        P(("replica", "tensor"), None),
        P("replica", "tensor", None),
        P(),
    )
    out_specs = (P("replica", "tensor", None), P("replica", "tensor", None), P("replica", "tensor"))
    return jax.shard_map(local, mesh=mesh, in_specs=in_specs, out_specs=out_specs, check_vma=False)
```

profile of v0, /device:TPU:130, one launch (start us, length us, event | category | flops | bytes accessed | tf_op | source)
XLA Modules:
  0.0 185.1 jit_solution(6643190026221381724)
XLA Ops:
  7.2 0.0 copy-start
  7.2 0.0 all-gather.2.cloned.1.call-start
  7.2 0.7 all-gather.2.cloned.1.call-update
  7.9 1.3 fusion.3
  10.5 111.9 %all-gather.2.cloned.1.call-done = bf16[1280,512]{1,0:T(8,128)(2,1)} async-done(((bf16[80,512]{1,0:T(8,128)(2,1)}), bf16[1280,512]{1,0:T(8,128)(2,1)}) %all-gather.2.cloned.1.call-update) | async-done | bytes 1310736 | tf_op jit(solution)/shard_map/all_gather | solution.py:29
  122.4 0.0 copy-done
  122.5 2.1 %fusion = f32[320,512]{1,0:T(8,128)S(1)} fusion(bf16[1280,320]{0,1:T(8,128)(2,1)S(1)} %copy-done, bf16[1280,512]{1,0:T(8,128)(2,1)} %all-gather.2.cloned.1.call-done, f32[1,320,512]{2,1,0:T(8,128)} %param.18), kind=kOutput, calls=%fused_computation.8 | convolution fusion | flops 419758080 | bytes 3440640 | tf_op jit(solution)/shard_map/dot_general | solution.py:30
  124.5 33.6 %conditional.2 = (f32[320,512]{1,0:T(8,128)S(1)}) conditional(s32[]{:T(128)} %bitcast.1, f32[320,512]{1,0:T(8,128)S(1)} %fusion, f32[320,512]{1,0:T(8,128)S(1)} %fusion, f32[320,512]{1,0:T(8,128)S(1)} %fusion, f32[320,512]{1,0:T(8,128)S(1)} %fusion, f32[320,512]{1,0:T(8,128)S(1)} %fusion, f32[320,512]{1,0:T(8,128)S(1)} %fusion), branch_computations={%region_0.0_spmd, %region_1.0_spmd, %region_2.0_spmd, %region_3.0_... | conditional | flops 327680 | bytes 4587568 | solution.py:21
  124.6 7.8 %collective-permute-start.11 = (f32[320,512]{1,0:T(8,128)S(1)}, f32[320,512]{1,0:T(8,128)S(1)}, u32[]{:S(2)}, u32[]{:S(2)}) collective-permute-start(f32[320,512]{1,0:T(8,128)S(1)} %param.5), channel_id=1, source_target_pairs={{0,512},{16,528},{32,544},{48,560},{64,576},{80,592},{96,608},{112... | collective-permute-start | bytes 1966088 | tf_op jit(solution)/shard_map/cond/branch_5_fun/ppermute | solution.py:12
  132.4 25.6 %collective-permute-done.11 = f32[320,512]{1,0:T(8,128)S(1)} collective-permute-done((f32[320,512]{1,0:T(8,128)S(1)}, f32[320,512]{1,0:T(8,128)S(1)}, u32[]{:S(2)}, u32[]{:S(2)}) %collective-permute-start.11) | collective-permute-done | bytes 655392 | tf_op jit(solution)/shard_map/cond/branch_5_fun/ppermute | solution.py:12
  158.0 0.1 add_multiply_fusion.5
  158.1 16.2 %conditional.3 = (f32[320,512]{1,0:T(8,128)S(1)}, f32[320,512]{1,0:T(8,128)S(1)}, f32[320,512]{1,0:T(8,128)}) conditional(s32[]{:T(128)} %bitcast, f32[320,512]{1,0:T(8,128)S(1)} %get-tuple-element.70, f32[320,512]{1,0:T(8,128)S(1)} %get-tuple-element.70, f32[320,512]{1,0:T(8,128)S(1)} %get-tuple-element.70, ...), branch_computations={%region_6.0_spmd, %region_7.0_spmd, %region_8.0_spmd, %region_9.0_... | conditional | bytes 3932224 | solution.py:21
  158.2 1.9 %collective-permute-start.1 = (f32[320,512]{1,0:T(8,128)S(1)}, f32[320,512]{1,0:T(8,128)}, u32[]{:S(2)}, u32[]{:S(2)}) collective-permute-start(f32[320,512]{1,0:T(8,128)S(1)} %param.7), channel_id=1, source_target_pairs={{0,32},{16,48},{32,0},{48,16},{64,96},{80,112},{96,64},{112,80},{1... | collective-permute-start | bytes 1966088 | tf_op jit(solution)/shard_map/cond/branch_1_fun/ppermute | solution.py:12
  160.1 14.2 %collective-permute-done.1 = f32[320,512]{1,0:T(8,128)} collective-permute-done((f32[320,512]{1,0:T(8,128)S(1)}, f32[320,512]{1,0:T(8,128)}, u32[]{:S(2)}, u32[]{:S(2)}) %collective-permute-start.1) | collective-permute-done | bytes 655392 | tf_op jit(solution)/shard_map/cond/branch_1_fun/ppermute | solution.py:12
  174.4 0.0 copy-start.1
  174.4 0.0 copy-start.2
  174.4 2.3 %convert_bitcast_fusion = (bf16[1,320,512]{2,1,0:T(8,128)(2,1)}, f32[1,320,512]{2,1,0:T(8,128)}) fusion(f32[320,512]{1,0:T(8,128)S(1)} %get-tuple-element.28, f32[320,512]{1,0:T(8,128)} %get-tuple-element.29), kind=kLoop, calls=%fused_computation.11 | loop fusion | flops 491520 | bytes 2293760 | tf_op jit(solution)/shard_map/broadcast_in_dim | solution.py:42
  176.7 0.0 copy-done.1
  176.7 0.0 copy-done.2
  176.7 1.5 fusion.4
  (1 shorter events, 0.0 us)
Async XLA Ops:
  7.2 115.3 %copy-start = (bf16[1280,320]{0,1:T(8,128)(2,1)S(1)}, bf16[1280,320]{0,1:T(8,128)(2,1)}, u32[]{:S(2)}) copy-start(bf16[1280,320]{0,1:T(8,128)(2,1)} %param.16) | copy-start | bytes 2457604
  7.2 115.3 %all-gather.2.cloned.1.call-start = ((), (), s32[]{:S(2)}) async-start(), calls=%async_computation | async-start | bytes 1392640 | tf_op jit(solution)/shard_map/all_gather | solution.py:29
  124.6 33.4 %collective-permute-start.11 = (f32[320,512]{1,0:T(8,128)S(1)}, f32[320,512]{1,0:T(8,128)S(1)}, u32[]{:S(2)}, u32[]{:S(2)}) collective-permute-start(f32[320,512]{1,0:T(8,128)S(1)} %param.5), channel_id=1, source_target_pairs={{0,512},{16,528},{32,544},{48,560},{64,576},{80,592},{96,608},{112... | collective-permute-start | bytes 1966088 | tf_op jit(solution)/shard_map/cond/branch_5_fun/ppermute | solution.py:12
  158.2 16.2 %collective-permute-start.1 = (f32[320,512]{1,0:T(8,128)S(1)}, f32[320,512]{1,0:T(8,128)}, u32[]{:S(2)}, u32[]{:S(2)}) collective-permute-start(f32[320,512]{1,0:T(8,128)S(1)} %param.7), channel_id=1, source_target_pairs={{0,32},{16,48},{32,0},{48,16},{64,96},{80,112},{96,64},{112,80},{1... | collective-permute-start | bytes 1966088 | tf_op jit(solution)/shard_map/cond/branch_1_fun/ppermute | solution.py:12
  174.4 2.3 %copy-start.1 = (bf16[1280,512]{1,0:T(8,128)(2,1)S(1)}, bf16[1280,512]{1,0:T(8,128)(2,1)}, u32[]{:S(2)}) copy-start(bf16[1280,512]{1,0:T(8,128)(2,1)} %all-gather.2.cloned.1.call-done) | copy-start | bytes 3932164
  174.4 2.3 %copy-start.2 = (f32[1,320,512]{2,1,0:T(8,128)S(1)}, f32[1,320,512]{2,1,0:T(8,128)}, u32[]{:S(2)}) copy-start(f32[1,320,512]{2,1,0:T(8,128)} %param.18) | copy-start | bytes 1966084
Sparse Core Ops, SparseCore 0:
  12.3 110.0 all-gather.1
where the time goes:
time: 185 us
  waiting for transfers between devices  152 us (82%)
  between operations  15.4 us (8%)
  starting transfers between devices  9.8 us (5%)
  matrix products  3.59 us (2%)
  other arithmetic  2.44 us (1%)
    all_gather x1, waiting for transfers between devices, local(): block_rows = lax.all_gather(key_grad, 'tensor', axis=0, tiled=True)  112 us
    ppermute x2, waiting for transfers between devices, from_partner(): lax.ppermute(shard, axis, [(i, i ^ 1 << bit) for i in range(lax.axis_size...  39.8 us
    ppermute x2, starting transfers between devices, from_partner(): lax.ppermute(shard, axis, [(i, i ^ 1 << bit) for i in range(lax.axis_size...  9.76 us
  transfers between devices with their start and end apart: 3, of which 3 were waited for; matrix products, arithmetic and copies ran while one was open for 1% of the time, Pallas kernels for 0%

commit v1 on v0

v1 whole, which is shorter than its diff:
```python
from functools import partial

import jax
import jax.numpy as jnp
from jax import lax
from jax.sharding import Mesh
from jax.sharding import PartitionSpec as P

step_rate = 0.2
BITS = ("r5", "r4", "r3", "r2", "r1", "r0")


def spread(block, axes, count):
    copies = jnp.broadcast_to(block[None], (count,) + block.shape)
    return lax.all_to_all(copies, axes, split_axis=0, concat_axis=0, tiled=True)


def swap(values, axis):
    return lax.ppermute(values, axis, [(0, 1), (1, 0)])


def swap_low(low_bit, values):
    return lax.switch(low_bit, [partial(swap, axis=BITS[5 - bit]) for bit in range(5)], values)


def shift(values, step):
    return lax.ppermute(values, "y", [(i, (i + step) % 8) for i in range(8)])


def gather_ring(block):
    me = lax.axis_index("y")
    right_x = lax.axis_index("x") == 1
    other = swap(block, "x")
    both = jnp.concatenate([jnp.where(right_x, other, block), jnp.where(right_x, block, other)], axis=0)
    rows = both.shape[0]
    whole = jnp.zeros((8 * rows, both.shape[1]), both.dtype)

    def put(whole, piece, source, offset=0):
        return lax.dynamic_update_slice(whole, piece, ((source % 8) * rows + offset, 0))

    whole = put(whole, both, me)
    up = down = both
    for step in range(1, 4):
        up, down = shift(up, 1), shift(down, -1)
        whole = put(put(whole, up, me - step), down, me + step)
    cut = rows // 2
    whole = put(whole, shift(up[:cut], 1), me + 4)
    return put(whole, shift(down[cut:], -1), me + 4, cut)


def local(features, key_grad, master, exponents):
    shard = master[0]
    working = shard.astype(jnp.bfloat16)
    block_rows = gather_ring(key_grad)
    weight_grad = lax.dot_general(
        features, block_rows, (((0,), (0,)), ((), ())), preferred_element_type=jnp.float32
    )
    stepped = shard - step_rate * weight_grad
    low_bit = jnp.minimum(exponents[0], exponents[1])
    upper = (lax.axis_index(BITS) >> low_bit) & 1 == 1
    half = stepped.shape[0] // 2
    top, bottom = stepped[:half], stepped[half:]
    given = jnp.where(upper, top, bottom).astype(jnp.bfloat16)
    kept = jnp.where(upper, bottom, top)
    pair = kept + swap_low(low_bit, given).astype(jnp.float32)
    other_pair = swap(pair.astype(jnp.bfloat16), "r5")
    mine = 0.25 * (pair + other_pair.astype(jnp.float32))
    rest = swap_low(low_bit, mine.astype(jnp.bfloat16)).astype(jnp.float32)
    mixed = jnp.concatenate([jnp.where(upper, rest, mine), jnp.where(upper, mine, rest)], axis=0)
    input_rows = lax.dot_general(
        block_rows, working, (((1,), (1,)), ((), ())), preferred_element_type=jnp.float32
    )
    return (mixed[None], mixed.astype(jnp.bfloat16)[None], input_rows.astype(jnp.bfloat16))


def solution(mesh):
    fine = Mesh(mesh.devices.reshape((2,) * 6 + (8, 2)), BITS + ("y", "x"))
    in_specs = (
        P(BITS, ("y", "x")),
        P(BITS + ("y", "x"), None),
        P(BITS, ("y", "x"), None),
        P(),
    )
    out_specs = (P(BITS, ("y", "x"), None), P(BITS, ("y", "x"), None), P(BITS, ("y", "x")))
    return jax.shard_map(local, mesh=fine, in_specs=in_specs, out_specs=out_specs, check_vma=False)
```

time: 185 us -> 103 us (0.56)
  the two profiles are of different devices: /device:TPU:130 before, /device:TPU:58 now
where the time goes in v1:
time: 103 us
  starting transfers between devices  62.9 us (61%)
  waiting for transfers between devices  28.7 us (28%)
  other arithmetic  4.64 us (5%)
  matrix products  3.2 us (3%)
  between operations  2.42 us (2%)
    ppermute x4, starting transfers between devices, swap(): return lax.ppermute(values, axis, [(0, 1), (1, 0)])  34.1 us
    ppermute x8, starting transfers between devices, shift(): return lax.ppermute(values, 'y', [(i, (i + step) % 8) for i in range(8)])  28.8 us
    ppermute x4, waiting for transfers between devices, swap(): return lax.ppermute(values, axis, [(0, 1), (1, 0)])  21.5 us
    ppermute x8, waiting for transfers between devices, shift(): return lax.ppermute(values, 'y', [(i, (i + step) % 8) for i in range(8)])  7.23 us
    dot_general x1, matrix products, local(): lax.dot_general(block_rows, working, (((1,), (1,)), ((), ())), preferred_...  2.61 us
  transfers between devices with their start and end apart: 12, of which 7 were waited for; matrix products, arithmetic and copies ran while one was open for 3% of the time, Pallas kernels for 0%

profile of v1, /device:TPU:58, one launch (start us, length us, event | category | flops | bytes accessed | tf_op | source)
XLA Modules:
  0.0 102.8 jit_solution(1072512043232689948)
XLA Ops:
  0.7 3.4 %collective-permute-start.10 = (bf16[80,512]{1,0:T(8,128)(2,1)}, bf16[80,512]{1,0:T(8,128)(2,1)S(1)}, u32[]{:S(2)}, u32[]{:S(2)}) collective-permute-start(bf16[80,512]{1,0:T(8,128)(2,1)} %param.15), channel_id=1, source_target_pairs={{0,1},{1,0},{2,3},{3,2},{4,5},{5,4},{6,7},{7,6},{8,9},{9,8},{10,11... | collective-permute-start | bytes 245768 | tf_op jit(solution)/shard_map/ppermute | solution.py:19
  4.1 7.9 %collective-permute-done.10 = bf16[80,512]{1,0:T(8,128)(2,1)S(1)} collective-permute-done((bf16[80,512]{1,0:T(8,128)(2,1)}, bf16[80,512]{1,0:T(8,128)(2,1)S(1)}, u32[]{:S(2)}, u32[]{:S(2)}) %collective-permute-start.10) | collective-permute-done | bytes 81952 | tf_op jit(solution)/shard_map/ppermute | solution.py:19
  12.0 0.9 broadcast_select_fusion.1
  12.9 0.1 broadcast_in_dim.7
  13.0 4.8 %collective-permute-start.11 = (bf16[160,512]{1,0:T(8,128)(2,1)S(1)}, bf16[160,512]{1,0:T(8,128)(2,1)S(1)}, u32[]{:S(2)}, u32[]{:S(2)}) collective-permute-start(bf16[160,512]{1,0:T(8,128)(2,1)S(1)} %get-tuple-element.45), channel_id=1, source_target_pairs={{0,2},{2,4},{4,6},{6,8},{8,10},{10,12},{12,14},{14,0},{1,3},{3,5},... | collective-permute-start | bytes 491528 | tf_op jit(solution)/shard_map/ppermute | solution.py:27
  17.8 1.9 %collective-permute-start.12 = (bf16[160,512]{1,0:T(8,128)(2,1)S(1)}, bf16[160,512]{1,0:T(8,128)(2,1)S(1)}, u32[]{:S(2)}, u32[]{:S(2)}) collective-permute-start(bf16[160,512]{1,0:T(8,128)(2,1)S(1)} %get-tuple-element.45), channel_id=1, source_target_pairs={{0,14},{2,0},{4,2},{6,4},{8,6},{10,8},{12,10},{14,12},{1,15},{3,1}... | collective-permute-start | bytes 491528 | tf_op jit(solution)/shard_map/ppermute | solution.py:27
  19.9 0.6 fusion.5
  21.9 5.1 %collective-permute-start.13 = (bf16[160,512]{1,0:T(8,128)(2,1)S(1)}, bf16[160,512]{1,0:T(8,128)(2,1)S(1)}, u32[]{:S(2)}, u32[]{:S(2)}) collective-permute-start(bf16[160,512]{1,0:T(8,128)(2,1)S(1)} %collective-permute-done.11), channel_id=1, source_target_pairs={{0,2},{2,4},{4,6},{6,8},{8,10},{10,12},{12,14},{14,0},{1,3},{3,5},... | collective-permute-start | bytes 491528 | tf_op jit(solution)/shard_map/ppermute | solution.py:27
  27.0 1.9 %collective-permute-start.14 = (bf16[160,512]{1,0:T(8,128)(2,1)S(1)}, bf16[160,512]{1,0:T(8,128)(2,1)S(1)}, u32[]{:S(2)}, u32[]{:S(2)}) collective-permute-start(bf16[160,512]{1,0:T(8,128)(2,1)S(1)} %collective-permute-done.12), channel_id=1, source_target_pairs={{0,14},{2,0},{4,2},{6,4},{8,6},{10,8},{12,10},{14,12},{1,15},{3,1}... | collective-permute-start | bytes 491528 | tf_op jit(solution)/shard_map/ppermute | solution.py:27
  29.0 0.8 collective-permute-done.13
  29.8 5.6 %collective-permute-start.15 = (bf16[160,512]{1,0:T(8,128)(2,1)S(1)}, bf16[160,512]{1,0:T(8,128)(2,1)S(1)}, u32[]{:S(2)}, u32[]{:S(2)}) collective-permute-start(bf16[160,512]{1,0:T(8,128)(2,1)S(1)} %collective-permute-done.13), channel_id=1, source_target_pairs={{0,2},{2,4},{4,6},{6,8},{8,10},{10,12},{12,14},{14,0},{1,3},{3,5},... | collective-permute-start | bytes 491528 | tf_op jit(solution)/shard_map/ppermute | solution.py:27
  35.5 1.9 %collective-permute-start.16 = (bf16[160,512]{1,0:T(8,128)(2,1)S(1)}, bf16[160,512]{1,0:T(8,128)(2,1)S(1)}, u32[]{:S(2)}, u32[]{:S(2)}) collective-permute-start(bf16[160,512]{1,0:T(8,128)(2,1)S(1)} %collective-permute-done.14), channel_id=1, source_target_pairs={{0,14},{2,0},{4,2},{6,4},{8,6},{10,8},{12,10},{14,12},{1,15},{3,1}... | collective-permute-start | bytes 491528 | tf_op jit(solution)/shard_map/ppermute | solution.py:27
  37.4 0.8 collective-permute-done.15
  38.3 5.6 %collective-permute-start.17 = (bf16[80,512]{1,0:T(8,128)(2,1)S(1)}, bf16[80,512]{1,0:T(8,128)(2,1)S(1)}, u32[]{:S(2)}, u32[]{:S(2)}) collective-permute-start(bf16[80,512]{1,0:T(8,128)(2,1)S(1)} %slice.24), channel_id=1, source_target_pairs={{0,2},{2,4},{4,6},{6,8},{8,10},{10,12},{12,14},{14,0},{1,3},{3,5},... | collective-permute-start | bytes 245768 | tf_op jit(solution)/shard_map/ppermute | solution.py:27
  43.9 0.0 collective-permute-done.16
  43.9 1.9 %collective-permute-start.18 = (bf16[80,512]{1,0:T(8,128)(2,1)S(1)}, bf16[80,512]{1,0:T(8,128)(2,1)S(1)}, u32[]{:S(2)}, u32[]{:S(2)}) collective-permute-start(bf16[80,512]{1,0:T(8,128)(2,1)S(1)} %slice.25), channel_id=1, source_target_pairs={{0,14},{2,0},{4,2},{6,4},{8,6},{10,8},{12,10},{14,12},{1,15},{3,1}... | collective-permute-start | bytes 245768 | tf_op jit(solution)/shard_map/ppermute | solution.py:27
  45.9 0.0 collective-permute-done.17
  45.9 5.5 %collective-permute-done.18 = bf16[80,512]{1,0:T(8,128)(2,1)S(1)} collective-permute-done((bf16[80,512]{1,0:T(8,128)(2,1)S(1)}, bf16[80,512]{1,0:T(8,128)(2,1)S(1)}, u32[]{:S(2)}, u32[]{:S(2)}) %collective-permute-start.18) | collective-permute-done | bytes 81952 | tf_op jit(solution)/shard_map/ppermute | solution.py:27
  51.5 0.6 fusion.1
  52.1 11.3 %conditional.8 = (bf16[160,512]{1,0:T(8,128)(2,1)}) conditional(s32[]{:T(128)} %clamp.4, bf16[160,512]{1,0:T(8,128)(2,1)S(1)} %select_convert_fusion, bf16[160,512]{1,0:T(8,128)(2,1)S(1)} %select_convert_fusion, bf16[160,512]{1,0:T(8,128)(2,1)S(1)} %select_convert_fusion, ...), branch_computations={%region_0.1_spmd, %region_1.2_spmd, %region_2.3_spmd, %region_3.4_... | conditional | bytes 655408
  52.1 7.9 %collective-permute-start.4 = (bf16[160,512]{1,0:T(8,128)(2,1)S(1)}, bf16[160,512]{1,0:T(8,128)(2,1)}, u32[]{:S(2)}, u32[]{:S(2)}) collective-permute-start(bf16[160,512]{1,0:T(8,128)(2,1)S(1)} %param.4), channel_id=1, source_target_pairs={{0,256},{256,0},{1,257},{257,1},{2,258},{258,2},{3,259},{259,3},{4... | collective-permute-start | bytes 491528 | tf_op jit(solution)/shard_map/cond/branch_4_fun/ppermute | solution.py:19
  60.0 3.4 %collective-permute-done.4 = bf16[160,512]{1,0:T(8,128)(2,1)} collective-permute-done((bf16[160,512]{1,0:T(8,128)(2,1)S(1)}, bf16[160,512]{1,0:T(8,128)(2,1)}, u32[]{:S(2)}, u32[]{:S(2)}) %collective-permute-start.4) | collective-permute-done | bytes 163872 | tf_op jit(solution)/shard_map/cond/branch_4_fun/ppermute | solution.py:19
  63.4 1.0 fusion.4
  64.4 20.9 %collective-permute-start.19 = (bf16[160,512]{1,0:T(8,128)(2,1)S(1)}, bf16[160,512]{1,0:T(8,128)(2,1)S(1)}, u32[]{:S(2)}, u32[]{:S(2)}) collective-permute-start(bf16[160,512]{1,0:T(8,128)(2,1)S(1)} %get-tuple-element.41), channel_id=1, source_target_pairs={{0,512},{512,0},{1,513},{513,1},{2,514},{514,2},{3,515},{515,3},{4... | collective-permute-start | bytes 491528 | tf_op jit(solution)/shard_map/ppermute | solution.py:19
  85.3 2.6 %fusion.6 = bf16[1280,320]{0,1:T(8,128)(2,1)} fusion(bf16[1280,512]{1,0:T(8,128)(2,1)S(1)} %constant_dynamic-update-slice_fusion, f32[1,320,512]{2,1,0:T(8,128)} %param.16), kind=kOutput, calls=%fused_computation.29 | convolution fusion | flops 419430400 | bytes 2785280 | tf_op jit(solution)/shard_map/dot_general | solution.py:70
  87.9 3.9 %collective-permute-done.19 = bf16[160,512]{1,0:T(8,128)(2,1)S(1)} collective-permute-done((bf16[160,512]{1,0:T(8,128)(2,1)S(1)}, bf16[160,512]{1,0:T(8,128)(2,1)S(1)}, u32[]{:S(2)}, u32[]{:S(2)}) %collective-permute-start.19) | collective-permute-done | bytes 163872 | tf_op jit(solution)/shard_map/ppermute | solution.py:19
  91.9 8.2 %conditional.9 = (bf16[160,512]{1,0:T(8,128)(2,1)}) conditional(s32[]{:T(128)} %clamp.4, bf16[160,512]{1,0:T(8,128)(2,1)S(1)} %fusion.2, bf16[160,512]{1,0:T(8,128)(2,1)S(1)} %fusion.2, bf16[160,512]{1,0:T(8,128)(2,1)S(1)} %fusion.2, bf16[160,512]{1,0:T(8,128)(2,1)S(1)} %fusion.2, bf16[160,512]{1,0:T(8,128)(2,1)S(1)} %fusion.2), branch_computations={%region_5.6_spmd, %region_6.7_spmd, %region_7.8_spmd, %region_8.9_... | conditional | bytes 655408
  91.9 1.9 %collective-permute-start.9 = (bf16[160,512]{1,0:T(8,128)(2,1)S(1)}, bf16[160,512]{1,0:T(8,128)(2,1)}, u32[]{:S(2)}, u32[]{:S(2)}) collective-permute-start(bf16[160,512]{1,0:T(8,128)(2,1)S(1)} %param.9), channel_id=1, source_target_pairs={{0,256},{256,0},{1,257},{257,1},{2,258},{258,2},{3,259},{259,3},{4... | collective-permute-start | bytes 491528 | tf_op jit(solution)/shard_map/cond/branch_4_fun/ppermute | solution.py:19
  93.8 6.3 %collective-permute-done.9 = bf16[160,512]{1,0:T(8,128)(2,1)} collective-permute-done((bf16[160,512]{1,0:T(8,128)(2,1)S(1)}, bf16[160,512]{1,0:T(8,128)(2,1)}, u32[]{:S(2)}, u32[]{:S(2)}) %collective-permute-start.9) | collective-permute-done | bytes 163872 | tf_op jit(solution)/shard_map/cond/branch_4_fun/ppermute | solution.py:19
  100.1 1.0 convert_bitcast_fusion.1
  101.1 0.7 pad_maximum_fusion
  101.9 0.9 maximum_bitcast_fusion
  (22 shorter events, 0.3 us)
Async XLA Ops:
  0.6 50.8 %copy-start = (bf16[1280,320]{0,1:T(8,128)(2,1)S(1)}, bf16[1280,320]{0,1:T(8,128)(2,1)}, u32[]{:S(2)}) copy-start(bf16[1280,320]{0,1:T(8,128)(2,1)} %param.14) | copy-start | bytes 2457604
  0.6 19.2 %copy-start.2 = (s32[2]{0:T(128)S(1)}, s32[2]{0:T(128)}, u32[]{:S(2)}) copy-start(s32[2]{0:T(128)} %param.17) | copy-start | bytes 28
  0.7 11.3 %collective-permute-start.10 = (bf16[80,512]{1,0:T(8,128)(2,1)}, bf16[80,512]{1,0:T(8,128)(2,1)S(1)}, u32[]{:S(2)}, u32[]{:S(2)}) collective-permute-start(bf16[80,512]{1,0:T(8,128)(2,1)} %param.15), channel_id=1, source_target_pairs={{0,1},{1,0},{2,3},{3,2},{4,5},{5,4},{6,7},{7,6},{8,9},{9,8},{10,11... | collective-permute-start | bytes 245768 | tf_op jit(solution)/shard_map/ppermute | solution.py:19
  13.0 8.8 %collective-permute-start.11 = (bf16[160,512]{1,0:T(8,128)(2,1)S(1)}, bf16[160,512]{1,0:T(8,128)(2,1)S(1)}, u32[]{:S(2)}, u32[]{:S(2)}) collective-permute-start(bf16[160,512]{1,0:T(8,128)(2,1)S(1)} %get-tuple-element.45), channel_id=1, source_target_pairs={{0,2},{2,4},{4,6},{6,8},{8,10},{10,12},{12,14},{14,0},{1,3},{3,5},... | collective-permute-start | bytes 491528 | tf_op jit(solution)/shard_map/ppermute | solution.py:27
  17.8 9.2 %collective-permute-start.12 = (bf16[160,512]{1,0:T(8,128)(2,1)S(1)}, bf16[160,512]{1,0:T(8,128)(2,1)S(1)}, u32[]{:S(2)}, u32[]{:S(2)}) collective-permute-start(bf16[160,512]{1,0:T(8,128)(2,1)S(1)} %get-tuple-element.45), channel_id=1, source_target_pairs={{0,14},{2,0},{4,2},{6,4},{8,6},{10,8},{12,10},{14,12},{1,15},{3,1}... | collective-permute-start | bytes 491528 | tf_op jit(solution)/shard_map/ppermute | solution.py:27
  21.9 8.0 %collective-permute-start.13 = (bf16[160,512]{1,0:T(8,128)(2,1)S(1)}, bf16[160,512]{1,0:T(8,128)(2,1)S(1)}, u32[]{:S(2)}, u32[]{:S(2)}) collective-permute-start(bf16[160,512]{1,0:T(8,128)(2,1)S(1)} %collective-permute-done.11), channel_id=1, source_target_pairs={{0,2},{2,4},{4,6},{6,8},{8,10},{10,12},{12,14},{14,0},{1,3},{3,5},... | collective-permute-start | bytes 491528 | tf_op jit(solution)/shard_map/ppermute | solution.py:27
  27.0 8.4 %collective-permute-start.14 = (bf16[160,512]{1,0:T(8,128)(2,1)S(1)}, bf16[160,512]{1,0:T(8,128)(2,1)S(1)}, u32[]{:S(2)}, u32[]{:S(2)}) collective-permute-start(bf16[160,512]{1,0:T(8,128)(2,1)S(1)} %collective-permute-done.12), channel_id=1, source_target_pairs={{0,14},{2,0},{4,2},{6,4},{8,6},{10,8},{12,10},{14,12},{1,15},{3,1}... | collective-permute-start | bytes 491528 | tf_op jit(solution)/shard_map/ppermute | solution.py:27
  28.9 22.5 %copy-start.1 = (f32[1,320,512]{2,1,0:T(8,128)S(1)}, f32[1,320,512]{2,1,0:T(8,128)}, u32[]{:S(2)}) copy-start(f32[1,320,512]{2,1,0:T(8,128)} %param.16) | copy-start | bytes 1966084
  29.8 8.4 %collective-permute-start.15 = (bf16[160,512]{1,0:T(8,128)(2,1)S(1)}, bf16[160,512]{1,0:T(8,128)(2,1)S(1)}, u32[]{:S(2)}, u32[]{:S(2)}) collective-permute-start(bf16[160,512]{1,0:T(8,128)(2,1)S(1)} %collective-permute-done.13), channel_id=1, source_target_pairs={{0,2},{2,4},{4,6},{6,8},{8,10},{10,12},{12,14},{14,0},{1,3},{3,5},... | collective-permute-start | bytes 491528 | tf_op jit(solution)/shard_map/ppermute | solution.py:27
  35.5 8.4 %collective-permute-start.16 = (bf16[160,512]{1,0:T(8,128)(2,1)S(1)}, bf16[160,512]{1,0:T(8,128)(2,1)S(1)}, u32[]{:S(2)}, u32[]{:S(2)}) collective-permute-start(bf16[160,512]{1,0:T(8,128)(2,1)S(1)} %collective-permute-done.14), channel_id=1, source_target_pairs={{0,14},{2,0},{4,2},{6,4},{8,6},{10,8},{12,10},{14,12},{1,15},{3,1}... | collective-permute-start | bytes 491528 | tf_op jit(solution)/shard_map/ppermute | solution.py:27
  38.3 7.6 %collective-permute-start.17 = (bf16[80,512]{1,0:T(8,128)(2,1)S(1)}, bf16[80,512]{1,0:T(8,128)(2,1)S(1)}, u32[]{:S(2)}, u32[]{:S(2)}) collective-permute-start(bf16[80,512]{1,0:T(8,128)(2,1)S(1)} %slice.24), channel_id=1, source_target_pairs={{0,2},{2,4},{4,6},{6,8},{8,10},{10,12},{12,14},{14,0},{1,3},{3,5},... | collective-permute-start | bytes 245768 | tf_op jit(solution)/shard_map/ppermute | solution.py:27
  43.9 7.5 %collective-permute-start.18 = (bf16[80,512]{1,0:T(8,128)(2,1)S(1)}, bf16[80,512]{1,0:T(8,128)(2,1)S(1)}, u32[]{:S(2)}, u32[]{:S(2)}) collective-permute-start(bf16[80,512]{1,0:T(8,128)(2,1)S(1)} %slice.25), channel_id=1, source_target_pairs={{0,14},{2,0},{4,2},{6,4},{8,6},{10,8},{12,10},{14,12},{1,15},{3,1}... | collective-permute-start | bytes 245768 | tf_op jit(solution)/shard_map/ppermute | solution.py:27
  52.1 11.3 %collective-permute-start.4 = (bf16[160,512]{1,0:T(8,128)(2,1)S(1)}, bf16[160,512]{1,0:T(8,128)(2,1)}, u32[]{:S(2)}, u32[]{:S(2)}) collective-permute-start(bf16[160,512]{1,0:T(8,128)(2,1)S(1)} %param.4), channel_id=1, source_target_pairs={{0,256},{256,0},{1,257},{257,1},{2,258},{258,2},{3,259},{259,3},{4... | collective-permute-start | bytes 491528 | tf_op jit(solution)/shard_map/cond/branch_4_fun/ppermute | solution.py:19
  64.4 27.4 %collective-permute-start.19 = (bf16[160,512]{1,0:T(8,128)(2,1)S(1)}, bf16[160,512]{1,0:T(8,128)(2,1)S(1)}, u32[]{:S(2)}, u32[]{:S(2)}) collective-permute-start(bf16[160,512]{1,0:T(8,128)(2,1)S(1)} %get-tuple-element.41), channel_id=1, source_target_pairs={{0,512},{512,0},{1,513},{513,1},{2,514},{514,2},{3,515},{515,3},{4... | collective-permute-start | bytes 491528 | tf_op jit(solution)/shard_map/ppermute | solution.py:19
  91.9 8.2 %collective-permute-start.9 = (bf16[160,512]{1,0:T(8,128)(2,1)S(1)}, bf16[160,512]{1,0:T(8,128)(2,1)}, u32[]{:S(2)}, u32[]{:S(2)}) collective-permute-start(bf16[160,512]{1,0:T(8,128)(2,1)S(1)} %param.9), channel_id=1, source_target_pairs={{0,256},{256,0},{1,257},{257,1},{2,258},{258,2},{3,259},{259,3},{4... | collective-permute-start | bytes 491528 | tf_op jit(solution)/shard_map/cond/branch_4_fun/ppermute | solution.py:19

commit v2 on v0

v2 whole, which is shorter than its diff:
```python
from functools import partial

import jax
import jax.numpy as jnp
from jax import lax
from jax.sharding import Mesh
from jax.sharding import PartitionSpec as P

step_rate = 0.2
BITS = ("r5", "r4", "r3", "r2", "r1", "r0")


def swap(values, axis):
    return lax.ppermute(values, axis, [(0, 1), (1, 0)])


EVEN = [(y, y ^ 1) for y in range(8)]
ODD = [(y, (((y + 1) ^ 1) - 1) % 8) for y in range(8)]


def gather(block, low_bit):
    rows, width = block.shape
    y, x = lax.axis_index("y"), lax.axis_index("x")
    ahead = jnp.where(y % 2 == 0, 1, -1)
    whole = jnp.zeros((16 * rows, width), block.dtype)

    def put(whole, pieces, side, sources):
        for number, source in enumerate(sources):
            piece = pieces[number * rows : (number + 1) * rows]
            whole = lax.dynamic_update_slice(whole, piece, (((source % 8) * 2 + side) * rows, 0))
        return whole

    near = jnp.where(y < 8, block, jnp.zeros_like(block))
    near, far, low_bit = lax.optimization_barrier((near, swap(block, "x"), low_bit))
    lanes = [(near, x, (EVEN, ODD), ahead), (far, 1 - x, (ODD, EVEN), -ahead)]
    for own, side, (first, second), d in lanes:
        one = lax.ppermute(own, "y", first)
        two = lax.ppermute(jnp.concatenate([own, one], axis=0), "y", second)
        three = lax.ppermute(two, "y", first)
        four = lax.ppermute(three, "y", second)
        whole = put(whole, own, side, [y])
        whole = put(whole, one, side, [y + d])
        whole = put(whole, two, side, [y - d, y - 2 * d])
        whole = put(whole, three, side, [y + 2 * d, y + 3 * d])
        whole = put(whole, four, side, [y - 3 * d, y - 4 * d])
    return whole, low_bit


def finish(shard, weight_grad, block_rows, low):
    stepped = shard - step_rate * weight_grad
    upper = lax.axis_index(low) == 1
    half = stepped.shape[0] // 2
    top, bottom = stepped[:half], stepped[half:]
    given = jnp.where(upper, top, bottom).astype(jnp.bfloat16)
    kept = lax.optimization_barrier(jnp.where(upper, bottom, top))
    pair = lax.optimization_barrier(kept + swap(given, low).astype(jnp.float32))
    other_pair = swap(pair.astype(jnp.bfloat16), "r5")
    input_rows = lax.dot_general(
        block_rows,
        shard.astype(jnp.bfloat16),
        (((1,), (1,)), ((), ())),
        preferred_element_type=jnp.float32,
    )
    other_pair, input_rows = lax.optimization_barrier((other_pair, input_rows.astype(jnp.bfloat16)))
    mine = 0.25 * (pair + other_pair.astype(jnp.float32))
    rest = swap(mine.astype(jnp.bfloat16), low).astype(jnp.float32)
    is_mine = (lax.broadcasted_iota(jnp.int32, (2, 1, 1), 0) == 1) == upper
    mixed = jnp.where(is_mine, mine[None], rest[None]).reshape(stepped.shape)
    return mixed[None], mixed.astype(jnp.bfloat16)[None], input_rows


def local(features, key_grad, master, exponents):
    shard = master[0]
    low_bit = jnp.minimum(exponents[0], exponents[1])
    block_rows, low_bit = gather(key_grad, low_bit)
    weight_grad = lax.dot_general(
        features, block_rows, (((0,), (0,)), ((), ())), preferred_element_type=jnp.float32
    )
    tails = [partial(finish, low=BITS[5 - bit]) for bit in range(5)]
    return lax.switch(low_bit, tails, shard, weight_grad, block_rows)


def solution(mesh):
    fine = Mesh(mesh.devices.reshape((2,) * 6 + (8, 2)), BITS + ("y", "x"))
    in_specs = (
        P(BITS, ("y", "x")),
        P(BITS + ("y", "x"), None),
        P(BITS, ("y", "x"), None),
        P(),
    )
    out_specs = (P(BITS, ("y", "x"), None), P(BITS, ("y", "x"), None), P(BITS, ("y", "x")))
    return jax.shard_map(local, mesh=fine, in_specs=in_specs, out_specs=out_specs, check_vma=False)
```

time: 185 us -> 88.7 us (0.48)
  the two profiles are of different devices: /device:TPU:130 before, /device:TPU:4 now
where the time goes in v2:
time: 88.7 us; the launch traced here: 88.1 us
  starting transfers between devices  51.5 us (58%)
  waiting for transfers between devices  27 us (30%)
  local copies, waits for them, and re-layouts  3.33 us (4%)
  between operations  2.62 us (3%)
  matrix products  2.1 us (2%)
  other arithmetic  1.43 us (2%)
    ppermute x4, starting transfers between devices, swap(): return lax.ppermute(values, axis, [(0, 1), (1, 0)])  24.2 us
    ppermute x4, waiting for transfers between devices, swap(): return lax.ppermute(values, axis, [(0, 1), (1, 0)])  15.5 us
    ppermute x2, starting transfers between devices, gather(): one = lax.ppermute(own, 'y', first)  10.3 us
    ppermute x2, starting transfers between devices, gather(): three = lax.ppermute(two, 'y', first)  8.43 us
    ppermute x2, waiting for transfers between devices, gather(): four = lax.ppermute(three, 'y', second)  5.08 us
    ppermute x2, starting transfers between devices, gather(): two = lax.ppermute(jnp.concatenate([own, one], axis=0), 'y', second)  4.7 us
    ppermute x2, starting transfers between devices, gather(): four = lax.ppermute(three, 'y', second)  3.83 us
    ppermute x2, waiting for transfers between devices, gather(): two = lax.ppermute(jnp.concatenate([own, one], axis=0), 'y', second)  3.53 us
  transfers between devices with their start and end apart: 12, of which 8 were waited for; matrix products, arithmetic and copies ran while one was open for 5% of the time, Pallas kernels for 0%

profile of v2, /device:TPU:4, one launch (start us, length us, event | category | flops | bytes accessed | tf_op | source)
XLA Modules:
  0.0 88.1 jit_solution(17361391699648957723)
XLA Ops:
  0.6 5.7 %collective-permute-start.15 = (bf16[80,512]{1,0:T(8,128)(2,1)}, bf16[80,512]{1,0:T(8,128)(2,1)S(1)}, u32[]{:S(2)}, u32[]{:S(2)}) collective-permute-start(bf16[80,512]{1,0:T(8,128)(2,1)} %param.10), channel_id=1, source_target_pairs={{0,1},{1,0},{2,3},{3,2},{4,5},{5,4},{6,7},{7,6},{8,9},{9,8},{10,11... | collective-permute-start | bytes 245768 | tf_op jit(solution)/shard_map/ppermute | solution.py:14
  6.4 0.9 %broadcast_select_fusion = bf16[80,512]{1,0:T(8,128)(2,1)S(1)} fusion(bf16[80,512]{1,0:T(8,128)(2,1)} %param.10, pred[]{:T(512)S(6)} %lt.119), kind=kLoop, calls=%fused_computation.60 | loop fusion | flops 40960 | bytes 163841 | tf_op jit(solution)/shard_map/jit(_where)/select_n | solution.py:33
  7.3 1.3 %fusion.15 = (s32[1]{0:T(128)}, s32[1]{0:T(128)}) fusion(s32[2]{0:T(128)} %param.12), kind=kLoop, calls=%fused_computation.75 | loop fusion | bytes 16 | tf_op jit(solution)/shard_map/slice | solution.py:74
  9.9 1.8 %collective-permute-done.15 = bf16[80,512]{1,0:T(8,128)(2,1)S(1)} collective-permute-done((bf16[80,512]{1,0:T(8,128)(2,1)}, bf16[80,512]{1,0:T(8,128)(2,1)S(1)}, u32[]{:S(2)}, u32[]{:S(2)}) %collective-permute-start.15) | collective-permute-done | bytes 81952 | tf_op jit(solution)/shard_map/ppermute | solution.py:14
  11.7 4.6 %collective-permute-start.16 = (bf16[80,512]{1,0:T(8,128)(2,1)S(1)}, bf16[80,512]{1,0:T(8,128)(2,1)S(1)}, u32[]{:S(2)}, u32[]{:S(2)}) collective-permute-start(bf16[80,512]{1,0:T(8,128)(2,1)S(1)} %broadcast_select_fusion), channel_id=1, source_target_pairs={{0,2},{2,0},{4,6},{6,4},{8,10},{10,8},{12,14},{14,12},{1,3},{3,1},... | collective-permute-start | bytes 245768 | tf_op jit(solution)/shard_map/ppermute | solution.py:37
  16.7 5.7 %collective-permute-start.20 = (bf16[80,512]{1,0:T(8,128)(2,1)S(1)}, bf16[80,512]{1,0:T(8,128)(2,1)S(1)}, u32[]{:S(2)}, u32[]{:S(2)}) collective-permute-start(bf16[80,512]{1,0:T(8,128)(2,1)S(1)} %collective-permute-done.15), channel_id=1, source_target_pairs={{0,14},{2,4},{4,2},{6,8},{8,6},{10,12},{12,10},{14,0},{1,15},{3,5}... | collective-permute-start | bytes 245768 | tf_op jit(solution)/shard_map/ppermute | solution.py:37
  22.5 2.8 %collective-permute-start.17 = (bf16[160,512]{1,0:T(8,128)(2,1)S(1)}, bf16[160,512]{1,0:T(8,128)(2,1)S(1)}, u32[]{:S(2)}, u32[]{:S(2)}) collective-permute-start(bf16[160,512]{1,0:T(8,128)(2,1)S(1)} %pad_maximum_fusion), channel_id=1, source_target_pairs={{0,14},{2,4},{4,2},{6,8},{8,6},{10,12},{12,10},{14,0},{1,15},{3,5}... | collective-permute-start | bytes 491528 | tf_op jit(solution)/shard_map/ppermute | solution.py:38
  25.3 1.9 %collective-permute-start.21 = (bf16[160,512]{1,0:T(8,128)(2,1)S(1)}, bf16[160,512]{1,0:T(8,128)(2,1)S(1)}, u32[]{:S(2)}, u32[]{:S(2)}) collective-permute-start(bf16[160,512]{1,0:T(8,128)(2,1)S(1)} %pad_maximum_fusion.1), channel_id=1, source_target_pairs={{0,2},{2,0},{4,6},{6,4},{8,10},{10,8},{12,14},{14,12},{1,3},{3,1},... | collective-permute-start | bytes 491528 | tf_op jit(solution)/shard_map/ppermute | solution.py:38
  27.3 0.1 broadcast_in_dim.146
  27.4 3.5 %collective-permute-done.17 = bf16[160,512]{1,0:T(8,128)(2,1)S(1)} collective-permute-done((bf16[160,512]{1,0:T(8,128)(2,1)S(1)}, bf16[160,512]{1,0:T(8,128)(2,1)S(1)}, u32[]{:S(2)}, u32[]{:S(2)}) %collective-permute-start.17) | collective-permute-done | bytes 163872 | tf_op jit(solution)/shard_map/ppermute | solution.py:38
  30.9 1.9 %collective-permute-start.18 = (bf16[160,512]{1,0:T(8,128)(2,1)S(1)}, bf16[160,512]{1,0:T(8,128)(2,1)S(1)}, u32[]{:S(2)}, u32[]{:S(2)}) collective-permute-start(bf16[160,512]{1,0:T(8,128)(2,1)S(1)} %collective-permute-done.17), channel_id=1, source_target_pairs={{0,2},{2,0},{4,6},{6,4},{8,10},{10,8},{12,14},{14,12},{1,3},{3,1},... | collective-permute-start | bytes 491528 | tf_op jit(solution)/shard_map/ppermute | solution.py:39
  32.9 6.5 %collective-permute-start.22 = (bf16[160,512]{1,0:T(8,128)(2,1)S(1)}, bf16[160,512]{1,0:T(8,128)(2,1)S(1)}, u32[]{:S(2)}, u32[]{:S(2)}) collective-permute-start(bf16[160,512]{1,0:T(8,128)(2,1)S(1)} %collective-permute-done.21), channel_id=1, source_target_pairs={{0,14},{2,4},{4,2},{6,8},{8,6},{10,12},{12,10},{14,0},{1,15},{3,5}... | collective-permute-start | bytes 491528 | tf_op jit(solution)/shard_map/ppermute | solution.py:39
  39.4 1.9 %collective-permute-start.19 = (bf16[160,512]{1,0:T(8,128)(2,1)S(1)}, bf16[160,512]{1,0:T(8,128)(2,1)S(1)}, u32[]{:S(2)}, u32[]{:S(2)}) collective-permute-start(bf16[160,512]{1,0:T(8,128)(2,1)S(1)} %collective-permute-done.18), channel_id=1, source_target_pairs={{0,14},{2,4},{4,2},{6,8},{8,6},{10,12},{12,10},{14,0},{1,15},{3,5}... | collective-permute-start | bytes 491528 | tf_op jit(solution)/shard_map/ppermute | solution.py:40
  41.4 2.9 %collective-permute-done.22 = bf16[160,512]{1,0:T(8,128)(2,1)S(1)} collective-permute-done((bf16[160,512]{1,0:T(8,128)(2,1)S(1)}, bf16[160,512]{1,0:T(8,128)(2,1)S(1)}, u32[]{:S(2)}, u32[]{:S(2)}) %collective-permute-start.22) | collective-permute-done | bytes 163872 | tf_op jit(solution)/shard_map/ppermute | solution.py:39
  44.2 1.9 %collective-permute-start.23 = (bf16[160,512]{1,0:T(8,128)(2,1)S(1)}, bf16[160,512]{1,0:T(8,128)(2,1)S(1)}, u32[]{:S(2)}, u32[]{:S(2)}) collective-permute-start(bf16[160,512]{1,0:T(8,128)(2,1)S(1)} %collective-permute-done.22), channel_id=1, source_target_pairs={{0,2},{2,0},{4,6},{6,4},{8,10},{10,8},{12,14},{14,12},{1,3},{3,1},... | collective-permute-start | bytes 491528 | tf_op jit(solution)/shard_map/ppermute | solution.py:40
  46.2 1.7 %collective-permute-done.19 = bf16[160,512]{1,0:T(8,128)(2,1)S(1)} collective-permute-done((bf16[160,512]{1,0:T(8,128)(2,1)S(1)}, bf16[160,512]{1,0:T(8,128)(2,1)S(1)}, u32[]{:S(2)}, u32[]{:S(2)}) %collective-permute-start.19) | collective-permute-done | bytes 163872 | tf_op jit(solution)/shard_map/ppermute | solution.py:40
  48.0 3.4 %collective-permute-done.23 = bf16[160,512]{1,0:T(8,128)(2,1)S(1)} collective-permute-done((bf16[160,512]{1,0:T(8,128)(2,1)S(1)}, bf16[160,512]{1,0:T(8,128)(2,1)S(1)}, u32[]{:S(2)}, u32[]{:S(2)}) %collective-permute-start.23) | collective-permute-done | bytes 163872 | tf_op jit(solution)/shard_map/ppermute | solution.py:40
  51.5 0.6 convolution_bitcast_fusion
  52.1 0.5 copy-done.1
  52.6 34.6 %conditional.4 = (f32[1,320,512]{2,1,0:T(8,128)S(1)}, bf16[1280,320]{0,1:T(8,128)(2,1)}, bf16[1,320,512]{2,1,0:T(8,128)(2,1)S(1)}) conditional(s32[]{:T(128)} %clamp.3, (f32[1,320,512]{2,1,0:T(8,128)S(1)}, f32[320,512]{1,0:T(8,128)S(1)}, bf16[1280,512]{1,0:T(8,128)(2,1)S(1)}) %tuple.86, ...), branch_computations={%region_0.1_spmd, %region_1.2_spmd, %region_2.3_spmd, %region_3.4_... | conditional | flops 420823040 | bytes 14583232
  52.6 0.1 bitcast_subtract_fusion.1
  52.7 1.9 %collective-permute-start.3 = (bf16[160,512]{1,0:T(8,128)(2,1)S(1)}, bf16[160,512]{1,0:T(8,128)(2,1)S(1)}, u32[]{:S(2)}, u32[]{:S(2)}) collective-permute-start(bf16[160,512]{1,0:T(8,128)(2,1)S(1)} %select_convert_fusion.1), channel_id=1, source_target_pairs={{0,32},{32,0},{1,33},{33,1},{2,34},{34,2},{3,35},{35,3},{4,36},{36... | collective-permute-start | bytes 491528 | tf_op jit(solution)/shard_map/cond/branch_1_fun/ppermute | solution.py:14
  54.7 5.2 %collective-permute-done.3 = bf16[160,512]{1,0:T(8,128)(2,1)S(1)} collective-permute-done((bf16[160,512]{1,0:T(8,128)(2,1)S(1)}, bf16[160,512]{1,0:T(8,128)(2,1)S(1)}, u32[]{:S(2)}, u32[]{:S(2)}) %collective-permute-start.3) | collective-permute-done | bytes 163872 | tf_op jit(solution)/shard_map/cond/branch_1_fun/ppermute | solution.py:14
  60.0 14.6 %collective-permute-start.4 = (bf16[160,512]{1,0:T(8,128)(2,1)S(1)}, bf16[160,512]{1,0:T(8,128)(2,1)S(1)}, u32[]{:S(2)}, u32[]{:S(2)}) collective-permute-start(bf16[160,512]{1,0:T(8,128)(2,1)S(1)} %convert_element_type.128), channel_id=1, source_target_pairs={{0,512},{512,0},{1,513},{513,1},{2,514},{514,2},{3,515},{515,3},{4... | collective-permute-start | bytes 491528 | tf_op jit(solution)/shard_map/cond/branch_1_fun/ppermute | solution.py:14
  74.6 1.5 %fusion.18 = bf16[1280,320]{0,1:T(8,128)(2,1)} fusion(bf16[1280,512]{1,0:T(8,128)(2,1)S(1)} %get-tuple-element.52, f32[1,320,512]{2,1,0:T(8,128)S(1)} %get-tuple-element.50), kind=kOutput, calls=%fused_computation.78 | convolution fusion | flops 419430400 | bytes 2785280 | tf_op jit(solution)/shard_map/cond/branch_1_fun/dot_general | solution.py:58
  76.1 3.5 %collective-permute-done.4 = bf16[160,512]{1,0:T(8,128)(2,1)S(1)} collective-permute-done((bf16[160,512]{1,0:T(8,128)(2,1)S(1)}, bf16[160,512]{1,0:T(8,128)(2,1)S(1)}, u32[]{:S(2)}, u32[]{:S(2)}) %collective-permute-start.4) | collective-permute-done | bytes 163872 | tf_op jit(solution)/shard_map/cond/branch_1_fun/ppermute | solution.py:14
  79.7 2.0 %collective-permute-start.5 = (bf16[160,512]{1,0:T(8,128)(2,1)S(1)}, bf16[160,512]{1,0:T(8,128)(2,1)S(1)}, u32[]{:S(2)}, u32[]{:S(2)}) collective-permute-start(bf16[160,512]{1,0:T(8,128)(2,1)S(1)} %get-tuple-element.96), channel_id=1, source_target_pairs={{0,32},{32,0},{1,33},{33,1},{2,34},{34,2},{3,35},{35,3},{4,36},{36... | collective-permute-start | bytes 491528 | tf_op jit(solution)/shard_map/cond/branch_1_fun/ppermute | solution.py:14
  81.8 0.1 broadcast_in_dim.116
  81.9 5.0 %collective-permute-done.5 = bf16[160,512]{1,0:T(8,128)(2,1)S(1)} collective-permute-done((bf16[160,512]{1,0:T(8,128)(2,1)S(1)}, bf16[160,512]{1,0:T(8,128)(2,1)S(1)}, u32[]{:S(2)}, u32[]{:S(2)}) %collective-permute-start.5) | collective-permute-done | bytes 163872 | tf_op jit(solution)/shard_map/cond/branch_1_fun/ppermute | solution.py:14
  87.0 0.1 fusion.7
  87.2 0.8 copy-done.2
  88.0 0.1 copy-done.3
  (36 shorter events, 0.7 us)
Async XLA Ops:
  0.6 50.8 %copy-start = (bf16[1280,320]{0,1:T(8,128)(2,1)S(1)}, bf16[1280,320]{0,1:T(8,128)(2,1)}, u32[]{:S(2)}) copy-start(bf16[1280,320]{0,1:T(8,128)(2,1)} %param.9) | copy-start | bytes 2457604
  0.6 11.1 %collective-permute-start.15 = (bf16[80,512]{1,0:T(8,128)(2,1)}, bf16[80,512]{1,0:T(8,128)(2,1)S(1)}, u32[]{:S(2)}, u32[]{:S(2)}) collective-permute-start(bf16[80,512]{1,0:T(8,128)(2,1)} %param.10), channel_id=1, source_target_pairs={{0,1},{1,0},{2,3},{3,2},{4,5},{5,4},{6,7},{7,6},{8,9},{9,8},{10,11... | collective-permute-start | bytes 245768 | tf_op jit(solution)/shard_map/ppermute | solution.py:14
  11.7 10.7 %collective-permute-start.16 = (bf16[80,512]{1,0:T(8,128)(2,1)S(1)}, bf16[80,512]{1,0:T(8,128)(2,1)S(1)}, u32[]{:S(2)}, u32[]{:S(2)}) collective-permute-start(bf16[80,512]{1,0:T(8,128)(2,1)S(1)} %broadcast_select_fusion), channel_id=1, source_target_pairs={{0,2},{2,0},{4,6},{6,4},{8,10},{10,8},{12,14},{14,12},{1,3},{3,1},... | collective-permute-start | bytes 245768 | tf_op jit(solution)/shard_map/ppermute | solution.py:37
  16.7 8.6 %collective-permute-start.20 = (bf16[80,512]{1,0:T(8,128)(2,1)S(1)}, bf16[80,512]{1,0:T(8,128)(2,1)S(1)}, u32[]{:S(2)}, u32[]{:S(2)}) collective-permute-start(bf16[80,512]{1,0:T(8,128)(2,1)S(1)} %collective-permute-done.15), channel_id=1, source_target_pairs={{0,14},{2,4},{4,2},{6,8},{8,6},{10,12},{12,10},{14,0},{1,15},{3,5}... | collective-permute-start | bytes 245768 | tf_op jit(solution)/shard_map/ppermute | solution.py:37
  22.5 8.4 %collective-permute-start.17 = (bf16[160,512]{1,0:T(8,128)(2,1)S(1)}, bf16[160,512]{1,0:T(8,128)(2,1)S(1)}, u32[]{:S(2)}, u32[]{:S(2)}) collective-permute-start(bf16[160,512]{1,0:T(8,128)(2,1)S(1)} %pad_maximum_fusion), channel_id=1, source_target_pairs={{0,14},{2,4},{4,2},{6,8},{8,6},{10,12},{12,10},{14,0},{1,15},{3,5}... | collective-permute-start | bytes 491528 | tf_op jit(solution)/shard_map/ppermute | solution.py:38
  25.3 7.5 %collective-permute-start.21 = (bf16[160,512]{1,0:T(8,128)(2,1)S(1)}, bf16[160,512]{1,0:T(8,128)(2,1)S(1)}, u32[]{:S(2)}, u32[]{:S(2)}) collective-permute-start(bf16[160,512]{1,0:T(8,128)(2,1)S(1)} %pad_maximum_fusion.1), channel_id=1, source_target_pairs={{0,2},{2,0},{4,6},{6,4},{8,10},{10,8},{12,14},{14,12},{1,3},{3,1},... | collective-permute-start | bytes 491528 | tf_op jit(solution)/shard_map/ppermute | solution.py:38
  30.9 8.5 %collective-permute-start.18 = (bf16[160,512]{1,0:T(8,128)(2,1)S(1)}, bf16[160,512]{1,0:T(8,128)(2,1)S(1)}, u32[]{:S(2)}, u32[]{:S(2)}) collective-permute-start(bf16[160,512]{1,0:T(8,128)(2,1)S(1)} %collective-permute-done.17), channel_id=1, source_target_pairs={{0,2},{2,0},{4,6},{6,4},{8,10},{10,8},{12,14},{14,12},{1,3},{3,1},... | collective-permute-start | bytes 491528 | tf_op jit(solution)/shard_map/ppermute | solution.py:39
  32.9 11.4 %collective-permute-start.22 = (bf16[160,512]{1,0:T(8,128)(2,1)S(1)}, bf16[160,512]{1,0:T(8,128)(2,1)S(1)}, u32[]{:S(2)}, u32[]{:S(2)}) collective-permute-start(bf16[160,512]{1,0:T(8,128)(2,1)S(1)} %collective-permute-done.21), channel_id=1, source_target_pairs={{0,14},{2,4},{4,2},{6,8},{8,6},{10,12},{12,10},{14,0},{1,15},{3,5}... | collective-permute-start | bytes 491528 | tf_op jit(solution)/shard_map/ppermute | solution.py:39
  39.4 8.4 %collective-permute-start.19 = (bf16[160,512]{1,0:T(8,128)(2,1)S(1)}, bf16[160,512]{1,0:T(8,128)(2,1)S(1)}, u32[]{:S(2)}, u32[]{:S(2)}) collective-permute-start(bf16[160,512]{1,0:T(8,128)(2,1)S(1)} %collective-permute-done.18), channel_id=1, source_target_pairs={{0,14},{2,4},{4,2},{6,8},{8,6},{10,12},{12,10},{14,0},{1,15},{3,5}... | collective-permute-start | bytes 491528 | tf_op jit(solution)/shard_map/ppermute | solution.py:40
  44.2 7.2 %collective-permute-start.23 = (bf16[160,512]{1,0:T(8,128)(2,1)S(1)}, bf16[160,512]{1,0:T(8,128)(2,1)S(1)}, u32[]{:S(2)}, u32[]{:S(2)}) collective-permute-start(bf16[160,512]{1,0:T(8,128)(2,1)S(1)} %collective-permute-done.22), channel_id=1, source_target_pairs={{0,2},{2,0},{4,6},{6,4},{8,10},{10,8},{12,14},{14,12},{1,3},{3,1},... | collective-permute-start | bytes 491528 | tf_op jit(solution)/shard_map/ppermute | solution.py:40
  51.5 1.1 %copy-start.1 = (f32[1,320,512]{2,1,0:T(8,128)S(1)}, f32[1,320,512]{2,1,0:T(8,128)}, u32[]{:S(2)}) copy-start(f32[1,320,512]{2,1,0:T(8,128)} %param.11) | copy-start | bytes 1966084
  52.7 7.2 %collective-permute-start.3 = (bf16[160,512]{1,0:T(8,128)(2,1)S(1)}, bf16[160,512]{1,0:T(8,128)(2,1)S(1)}, u32[]{:S(2)}, u32[]{:S(2)}) collective-permute-start(bf16[160,512]{1,0:T(8,128)(2,1)S(1)} %select_convert_fusion.1), channel_id=1, source_target_pairs={{0,32},{32,0},{1,33},{33,1},{2,34},{34,2},{3,35},{35,3},{4,36},{36... | collective-permute-start | bytes 491528 | tf_op jit(solution)/shard_map/cond/branch_1_fun/ppermute | solution.py:14
  60.0 19.6 %collective-permute-start.4 = (bf16[160,512]{1,0:T(8,128)(2,1)S(1)}, bf16[160,512]{1,0:T(8,128)(2,1)S(1)}, u32[]{:S(2)}, u32[]{:S(2)}) collective-permute-start(bf16[160,512]{1,0:T(8,128)(2,1)S(1)} %convert_element_type.128), channel_id=1, source_target_pairs={{0,512},{512,0},{1,513},{513,1},{2,514},{514,2},{3,515},{515,3},{4... | collective-permute-start | bytes 491528 | tf_op jit(solution)/shard_map/cond/branch_1_fun/ppermute | solution.py:14
  79.7 7.2 %collective-permute-start.5 = (bf16[160,512]{1,0:T(8,128)(2,1)S(1)}, bf16[160,512]{1,0:T(8,128)(2,1)S(1)}, u32[]{:S(2)}, u32[]{:S(2)}) collective-permute-start(bf16[160,512]{1,0:T(8,128)(2,1)S(1)} %get-tuple-element.96), channel_id=1, source_target_pairs={{0,32},{32,0},{1,33},{33,1},{2,34},{34,2},{3,35},{35,3},{4,36},{36... | collective-permute-start | bytes 491528 | tf_op jit(solution)/shard_map/cond/branch_1_fun/ppermute | solution.py:14
  87.2 0.8 copy-start.2
  87.2 0.9 %copy-start.3 = (bf16[1,320,512]{2,1,0:T(8,128)(2,1)}, bf16[1,320,512]{2,1,0:T(8,128)(2,1)S(1)}, u32[]{:S(2)}) copy-start(bf16[1,320,512]{2,1,0:T(8,128)(2,1)S(1)} %get-tuple-element.89) | copy-start | bytes 983044

commit v3 on v2

--- a/solution.py
+++ b/solution.py
@@ -69,6 +69,27 @@
     return mixed[None], mixed.astype(jnp.bfloat16)[None], input_rows
 
 
+def finish_four(shard, weight_grad, block_rows, low):
+    stepped = shard - step_rate * weight_grad
+    rows, width = stepped.shape
+    axes = ("r5", low)
+    input_rows = lax.dot_general(
+        block_rows,
+        shard.astype(jnp.bfloat16),
+        (((1,), (1,)), ((), ())),
+        preferred_element_type=jnp.float32,
+    ).astype(jnp.bfloat16)
+    pieces = stepped.astype(jnp.bfloat16).reshape(4, rows // 4, width)
+    arrived = lax.all_to_all(pieces, axes, split_axis=0, concat_axis=0, tiled=True)
+    arrived, input_rows = lax.optimization_barrier((arrived, input_rows))
+    mine = 0.25 * jnp.sum(arrived.astype(jnp.float32), axis=0)
+    copies = jnp.broadcast_to(mine.astype(jnp.bfloat16)[None], pieces.shape)
+    back = lax.all_to_all(copies, axes, split_axis=0, concat_axis=0, tiled=True)
+    is_mine = lax.broadcasted_iota(jnp.int32, (4, 1, 1), 0) == lax.axis_index(axes)
+    mixed = jnp.where(is_mine, mine[None], back.astype(jnp.float32)).reshape(stepped.shape)
+    return mixed[None], mixed.astype(jnp.bfloat16)[None], input_rows
+
+
 def local(features, key_grad, master, exponents):
     shard = master[0]
     low_bit = jnp.minimum(exponents[0], exponents[1])
@@ -76,7 +97,8 @@
     weight_grad = lax.dot_general(
         features, block_rows, (((0,), (0,)), ((), ())), preferred_element_type=jnp.float32
     )
-    tails = [partial(finish, low=BITS[5 - bit]) for bit in range(5)]
+    forms = (finish, finish, finish, finish, finish_four)
+    tails = [partial(form, low=BITS[5 - bit]) for bit, form in enumerate(forms)]
     return lax.switch(low_bit, tails, shard, weight_grad, block_rows)
 
 

time: 88.7 us -> 90.4 us (1.019)
  the two profiles are of different devices: /device:TPU:4 before, /device:TPU:12 now
where the time goes in v3:
time: 90.4 us; the launch traced here: 89.8 us
  starting transfers between devices  51.7 us (57%)
  waiting for transfers between devices  28 us (31%)
  local copies, waits for them, and re-layouts  3.12 us (3%)
  between operations  2.58 us (3%)
  other arithmetic  2.27 us (3%)
  matrix products  2.1 us (2%)
    ppermute x4, starting transfers between devices, swap(): return lax.ppermute(values, axis, [(0, 1), (1, 0)])  26.7 us
    ppermute x4, waiting for transfers between devices, swap(): return lax.ppermute(values, axis, [(0, 1), (1, 0)])  15 us
    ppermute x2, starting transfers between devices, gather(): one = lax.ppermute(own, 'y', first)  10.3 us
    ppermute x2, waiting for transfers between devices, gather(): four = lax.ppermute(three, 'y', second)  5.08 us
    ppermute x2, starting transfers between devices, gather(): four = lax.ppermute(three, 'y', second)  5.03 us
    ppermute x2, starting transfers between devices, gather(): three = lax.ppermute(two, 'y', first)  4.99 us
    ppermute x2, waiting for transfers between devices, gather(): two = lax.ppermute(jnp.concatenate([own, one], axis=0), 'y', second)  4.83 us
    ppermute x2, starting transfers between devices, gather(): two = lax.ppermute(jnp.concatenate([own, one], axis=0), 'y', second)  4.7 us
  transfers between devices with their start and end apart: 12, of which 10 were waited for; matrix products, arithmetic and copies ran while one was open for 5% of the time, Pallas kernels for 0%

profile of v3, /device:TPU:12, one launch (start us, length us, event | category | flops | bytes accessed | tf_op | source)
XLA Modules:
  0.0 89.8 jit_solution(4619646914692099159)
XLA Ops:
  0.6 4.3 %collective-permute-start.12 = (bf16[80,512]{1,0:T(8,128)(2,1)}, bf16[80,512]{1,0:T(8,128)(2,1)S(1)}, u32[]{:S(2)}, u32[]{:S(2)}) collective-permute-start(bf16[80,512]{1,0:T(8,128)(2,1)} %param.10), channel_id=1, source_target_pairs={{0,1},{1,0},{2,3},{3,2},{4,5},{5,4},{6,7},{7,6},{8,9},{9,8},{10,11... | collective-permute-start | bytes 245768 | tf_op jit(solution)/shard_map/ppermute | solution.py:14
  4.9 0.9 %broadcast_select_fusion = bf16[80,512]{1,0:T(8,128)(2,1)S(1)} fusion(bf16[80,512]{1,0:T(8,128)(2,1)} %param.10, pred[]{:T(512)S(6)} %lt.119), kind=kLoop, calls=%fused_computation.60 | loop fusion | flops 40960 | bytes 163841 | tf_op jit(solution)/shard_map/jit(_where)/select_n | solution.py:33
  5.9 1.3 %fusion.15 = (s32[1]{0:T(128)}, s32[1]{0:T(128)}) fusion(s32[2]{0:T(128)} %param.12), kind=kLoop, calls=%fused_computation.73 | loop fusion | bytes 16 | tf_op jit(solution)/shard_map/slice | solution.py:95
  8.5 3.4 %collective-permute-done.12 = bf16[80,512]{1,0:T(8,128)(2,1)S(1)} collective-permute-done((bf16[80,512]{1,0:T(8,128)(2,1)}, bf16[80,512]{1,0:T(8,128)(2,1)S(1)}, u32[]{:S(2)}, u32[]{:S(2)}) %collective-permute-start.12) | collective-permute-done | bytes 81952 | tf_op jit(solution)/shard_map/ppermute | solution.py:14
  11.9 4.5 %collective-permute-start.13 = (bf16[80,512]{1,0:T(8,128)(2,1)S(1)}, bf16[80,512]{1,0:T(8,128)(2,1)S(1)}, u32[]{:S(2)}, u32[]{:S(2)}) collective-permute-start(bf16[80,512]{1,0:T(8,128)(2,1)S(1)} %broadcast_select_fusion), channel_id=1, source_target_pairs={{0,2},{2,0},{4,6},{6,4},{8,10},{10,8},{12,14},{14,12},{1,3},{3,1},... | collective-permute-start | bytes 245768 | tf_op jit(solution)/shard_map/ppermute | solution.py:37
  16.8 5.7 %collective-permute-start.17 = (bf16[80,512]{1,0:T(8,128)(2,1)S(1)}, bf16[80,512]{1,0:T(8,128)(2,1)S(1)}, u32[]{:S(2)}, u32[]{:S(2)}) collective-permute-start(bf16[80,512]{1,0:T(8,128)(2,1)S(1)} %collective-permute-done.12), channel_id=1, source_target_pairs={{0,14},{2,4},{4,2},{6,8},{8,6},{10,12},{12,10},{14,0},{1,15},{3,5}... | collective-permute-start | bytes 245768 | tf_op jit(solution)/shard_map/ppermute | solution.py:37
  22.6 2.8 %collective-permute-start.14 = (bf16[160,512]{1,0:T(8,128)(2,1)S(1)}, bf16[160,512]{1,0:T(8,128)(2,1)S(1)}, u32[]{:S(2)}, u32[]{:S(2)}) collective-permute-start(bf16[160,512]{1,0:T(8,128)(2,1)S(1)} %pad_maximum_fusion), channel_id=1, source_target_pairs={{0,14},{2,4},{4,2},{6,8},{8,6},{10,12},{12,10},{14,0},{1,15},{3,5}... | collective-permute-start | bytes 491528 | tf_op jit(solution)/shard_map/ppermute | solution.py:38
  25.4 1.9 %collective-permute-start.18 = (bf16[160,512]{1,0:T(8,128)(2,1)S(1)}, bf16[160,512]{1,0:T(8,128)(2,1)S(1)}, u32[]{:S(2)}, u32[]{:S(2)}) collective-permute-start(bf16[160,512]{1,0:T(8,128)(2,1)S(1)} %pad_maximum_fusion.1), channel_id=1, source_target_pairs={{0,2},{2,0},{4,6},{6,4},{8,10},{10,8},{12,14},{14,12},{1,3},{3,1},... | collective-permute-start | bytes 491528 | tf_op jit(solution)/shard_map/ppermute | solution.py:38
  27.4 0.1 broadcast_in_dim.144
  27.5 3.5 %collective-permute-done.14 = bf16[160,512]{1,0:T(8,128)(2,1)S(1)} collective-permute-done((bf16[160,512]{1,0:T(8,128)(2,1)S(1)}, bf16[160,512]{1,0:T(8,128)(2,1)S(1)}, u32[]{:S(2)}, u32[]{:S(2)}) %collective-permute-start.14) | collective-permute-done | bytes 163872 | tf_op jit(solution)/shard_map/ppermute | solution.py:38
  31.0 1.9 %collective-permute-start.15 = (bf16[160,512]{1,0:T(8,128)(2,1)S(1)}, bf16[160,512]{1,0:T(8,128)(2,1)S(1)}, u32[]{:S(2)}, u32[]{:S(2)}) collective-permute-start(bf16[160,512]{1,0:T(8,128)(2,1)S(1)} %collective-permute-done.14), channel_id=1, source_target_pairs={{0,2},{2,0},{4,6},{6,4},{8,10},{10,8},{12,14},{14,12},{1,3},{3,1},... | collective-permute-start | bytes 491528 | tf_op jit(solution)/shard_map/ppermute | solution.py:39
  32.9 1.3 %collective-permute-done.18 = bf16[160,512]{1,0:T(8,128)(2,1)S(1)} collective-permute-done((bf16[160,512]{1,0:T(8,128)(2,1)S(1)}, bf16[160,512]{1,0:T(8,128)(2,1)S(1)}, u32[]{:S(2)}, u32[]{:S(2)}) %collective-permute-start.18) | collective-permute-done | bytes 163872 | tf_op jit(solution)/shard_map/ppermute | solution.py:38
  34.2 3.1 %collective-permute-start.19 = (bf16[160,512]{1,0:T(8,128)(2,1)S(1)}, bf16[160,512]{1,0:T(8,128)(2,1)S(1)}, u32[]{:S(2)}, u32[]{:S(2)}) collective-permute-start(bf16[160,512]{1,0:T(8,128)(2,1)S(1)} %collective-permute-done.18), channel_id=1, source_target_pairs={{0,14},{2,4},{4,2},{6,8},{8,6},{10,12},{12,10},{14,0},{1,15},{3,5}... | collective-permute-start | bytes 491528 | tf_op jit(solution)/shard_map/ppermute | solution.py:39
  37.4 0.9 collective-permute-done.15
  38.2 3.1 %collective-permute-start.16 = (bf16[160,512]{1,0:T(8,128)(2,1)S(1)}, bf16[160,512]{1,0:T(8,128)(2,1)S(1)}, u32[]{:S(2)}, u32[]{:S(2)}) collective-permute-start(bf16[160,512]{1,0:T(8,128)(2,1)S(1)} %collective-permute-done.15), channel_id=1, source_target_pairs={{0,14},{2,4},{4,2},{6,8},{8,6},{10,12},{12,10},{14,0},{1,15},{3,5}... | collective-permute-start | bytes 491528 | tf_op jit(solution)/shard_map/ppermute | solution.py:40
  41.4 2.2 %collective-permute-done.19 = bf16[160,512]{1,0:T(8,128)(2,1)S(1)} collective-permute-done((bf16[160,512]{1,0:T(8,128)(2,1)S(1)}, bf16[160,512]{1,0:T(8,128)(2,1)S(1)}, u32[]{:S(2)}, u32[]{:S(2)}) %collective-permute-start.19) | collective-permute-done | bytes 163872 | tf_op jit(solution)/shard_map/ppermute | solution.py:39
  43.6 1.9 %collective-permute-start.20 = (bf16[160,512]{1,0:T(8,128)(2,1)S(1)}, bf16[160,512]{1,0:T(8,128)(2,1)S(1)}, u32[]{:S(2)}, u32[]{:S(2)}) collective-permute-start(bf16[160,512]{1,0:T(8,128)(2,1)S(1)} %collective-permute-done.19), channel_id=1, source_target_pairs={{0,2},{2,0},{4,6},{6,4},{8,10},{10,8},{12,14},{14,12},{1,3},{3,1},... | collective-permute-start | bytes 491528 | tf_op jit(solution)/shard_map/ppermute | solution.py:40
  45.5 1.1 %collective-permute-done.16 = bf16[160,512]{1,0:T(8,128)(2,1)S(1)} collective-permute-done((bf16[160,512]{1,0:T(8,128)(2,1)S(1)}, bf16[160,512]{1,0:T(8,128)(2,1)S(1)}, u32[]{:S(2)}, u32[]{:S(2)}) %collective-permute-start.16) | collective-permute-done | bytes 163872 | tf_op jit(solution)/shard_map/ppermute | solution.py:40
  46.8 4.0 %collective-permute-done.20 = bf16[160,512]{1,0:T(8,128)(2,1)S(1)} collective-permute-done((bf16[160,512]{1,0:T(8,128)(2,1)S(1)}, bf16[160,512]{1,0:T(8,128)(2,1)S(1)}, u32[]{:S(2)}, u32[]{:S(2)}) %collective-permute-start.20) | collective-permute-done | bytes 163872 | tf_op jit(solution)/shard_map/ppermute | solution.py:40
  50.8 0.6 convolution_bitcast_fusion
  51.4 0.5 copy-done.1
  51.9 37.2 %conditional.4 = (f32[1,320,512]{2,1,0:T(8,128)}, bf16[1280,320]{0,1:T(8,128)(2,1)}, bf16[1,320,512]{2,1,0:T(8,128)(2,1)S(1)}) conditional(s32[]{:T(128)} %clamp.3, (f32[1,320,512]{2,1,0:T(8,128)S(1)}, f32[320,512]{1,0:T(8,128)S(1)}, bf16[1280,512]{1,0:T(8,128)(2,1)S(1)}) %tuple.85, (f32[1,320,512]{2,1,0:T(8,128)S(1)}, ...), branch_computations={%region_0.1_spmd, %region_1.2_spmd, %region_2.3_spmd, %region_3.4_... | conditional | flops 420823040 | bytes 14583232
  51.9 0.1 bitcast_subtract_fusion.3
  52.1 5.2 %collective-permute-start.9 = (bf16[160,512]{1,0:T(8,128)(2,1)S(1)}, bf16[160,512]{1,0:T(8,128)(2,1)S(1)}, u32[]{:S(2)}, u32[]{:S(2)}) collective-permute-start(bf16[160,512]{1,0:T(8,128)(2,1)S(1)} %select_convert_fusion.3), channel_id=1, source_target_pairs={{0,128},{128,0},{1,129},{129,1},{2,130},{130,2},{3,131},{131,3},{4... | collective-permute-start | bytes 491528 | tf_op jit(solution)/shard_map/cond/branch_3_fun/ppermute | solution.py:14
  57.3 3.2 %collective-permute-done.9 = bf16[160,512]{1,0:T(8,128)(2,1)S(1)} collective-permute-done((bf16[160,512]{1,0:T(8,128)(2,1)S(1)}, bf16[160,512]{1,0:T(8,128)(2,1)S(1)}, u32[]{:S(2)}, u32[]{:S(2)}) %collective-permute-start.9) | collective-permute-done | bytes 163872 | tf_op jit(solution)/shard_map/cond/branch_3_fun/ppermute | solution.py:14
  60.6 14.1 %collective-permute-start.10 = (bf16[160,512]{1,0:T(8,128)(2,1)S(1)}, bf16[160,512]{1,0:T(8,128)(2,1)S(1)}, u32[]{:S(2)}, u32[]{:S(2)}) collective-permute-start(bf16[160,512]{1,0:T(8,128)(2,1)S(1)} %convert_element_type.146), channel_id=1, source_target_pairs={{0,512},{512,0},{1,513},{513,1},{2,514},{514,2},{3,515},{515,3},{4... | collective-permute-start | bytes 491528 | tf_op jit(solution)/shard_map/cond/branch_3_fun/ppermute | solution.py:14
  74.7 1.5 %fusion.24 = bf16[1280,320]{0,1:T(8,128)(2,1)} fusion(bf16[1280,512]{1,0:T(8,128)(2,1)S(1)} %get-tuple-element.62, f32[1,320,512]{2,1,0:T(8,128)S(1)} %get-tuple-element.60), kind=kOutput, calls=%fused_computation.82 | convolution fusion | flops 419430400 | bytes 2785280 | tf_op jit(solution)/shard_map/cond/branch_3_fun/dot_general | solution.py:58
  76.3 4.5 %collective-permute-done.10 = bf16[160,512]{1,0:T(8,128)(2,1)S(1)} collective-permute-done((bf16[160,512]{1,0:T(8,128)(2,1)S(1)}, bf16[160,512]{1,0:T(8,128)(2,1)S(1)}, u32[]{:S(2)}, u32[]{:S(2)}) %collective-permute-start.10) | collective-permute-done | bytes 163872 | tf_op jit(solution)/shard_map/cond/branch_3_fun/ppermute | solution.py:14
  80.8 3.1 %collective-permute-start.11 = (bf16[160,512]{1,0:T(8,128)(2,1)S(1)}, bf16[160,512]{1,0:T(8,128)(2,1)S(1)}, u32[]{:S(2)}, u32[]{:S(2)}) collective-permute-start(bf16[160,512]{1,0:T(8,128)(2,1)S(1)} %get-tuple-element.104), channel_id=1, source_target_pairs={{0,128},{128,0},{1,129},{129,1},{2,130},{130,2},{3,131},{131,3},{4... | collective-permute-start | bytes 491528 | tf_op jit(solution)/shard_map/cond/branch_3_fun/ppermute | solution.py:14
  84.1 3.9 %collective-permute-done.11 = bf16[160,512]{1,0:T(8,128)(2,1)S(1)} collective-permute-done((bf16[160,512]{1,0:T(8,128)(2,1)S(1)}, bf16[160,512]{1,0:T(8,128)(2,1)S(1)}, u32[]{:S(2)}, u32[]{:S(2)}) %collective-permute-start.11) | collective-permute-done | bytes 163872 | tf_op jit(solution)/shard_map/cond/branch_3_fun/ppermute | solution.py:14
  88.1 1.0 %fusion.13 = (bf16[1,320,512]{2,1,0:T(8,128)(2,1)S(1)}, f32[1,320,512]{2,1,0:T(8,128)}) fusion(pred[320]{0:T(512)(128)(4,1)S(1)} %broadcast_in_dim.132, f32[1,320,512]{2,1,0:T(8,128)S(1)} %bitcast.108, f32[1,320,512]{2,1,0:T(8,128)S(1)} %bitcast.112), kind=kLoop, calls=%fused_computation.71 | loop fusion | flops 327680 | bytes 2294080 | tf_op jit(solution)/shard_map/cond/branch_0_fun/convert_element_type | solution.py:69
  89.1 0.7 copy-done.2
  (34 shorter events, 0.7 us)
Async XLA Ops:
  0.6 50.2 %copy-start = (bf16[1280,320]{0,1:T(8,128)(2,1)S(1)}, bf16[1280,320]{0,1:T(8,128)(2,1)}, u32[]{:S(2)}) copy-start(bf16[1280,320]{0,1:T(8,128)(2,1)} %param.9) | copy-start | bytes 2457604
  0.6 11.3 %collective-permute-start.12 = (bf16[80,512]{1,0:T(8,128)(2,1)}, bf16[80,512]{1,0:T(8,128)(2,1)S(1)}, u32[]{:S(2)}, u32[]{:S(2)}) collective-permute-start(bf16[80,512]{1,0:T(8,128)(2,1)} %param.10), channel_id=1, source_target_pairs={{0,1},{1,0},{2,3},{3,2},{4,5},{5,4},{6,7},{7,6},{8,9},{9,8},{10,11... | collective-permute-start | bytes 245768 | tf_op jit(solution)/shard_map/ppermute | solution.py:14
  11.9 10.7 %collective-permute-start.13 = (bf16[80,512]{1,0:T(8,128)(2,1)S(1)}, bf16[80,512]{1,0:T(8,128)(2,1)S(1)}, u32[]{:S(2)}, u32[]{:S(2)}) collective-permute-start(bf16[80,512]{1,0:T(8,128)(2,1)S(1)} %broadcast_select_fusion), channel_id=1, source_target_pairs={{0,2},{2,0},{4,6},{6,4},{8,10},{10,8},{12,14},{14,12},{1,3},{3,1},... | collective-permute-start | bytes 245768 | tf_op jit(solution)/shard_map/ppermute | solution.py:37
  16.8 8.6 %collective-permute-start.17 = (bf16[80,512]{1,0:T(8,128)(2,1)S(1)}, bf16[80,512]{1,0:T(8,128)(2,1)S(1)}, u32[]{:S(2)}, u32[]{:S(2)}) collective-permute-start(bf16[80,512]{1,0:T(8,128)(2,1)S(1)} %collective-permute-done.12), channel_id=1, source_target_pairs={{0,14},{2,4},{4,2},{6,8},{8,6},{10,12},{12,10},{14,0},{1,15},{3,5}... | collective-permute-start | bytes 245768 | tf_op jit(solution)/shard_map/ppermute | solution.py:37
  22.6 8.4 %collective-permute-start.14 = (bf16[160,512]{1,0:T(8,128)(2,1)S(1)}, bf16[160,512]{1,0:T(8,128)(2,1)S(1)}, u32[]{:S(2)}, u32[]{:S(2)}) collective-permute-start(bf16[160,512]{1,0:T(8,128)(2,1)S(1)} %pad_maximum_fusion), channel_id=1, source_target_pairs={{0,14},{2,4},{4,2},{6,8},{8,6},{10,12},{12,10},{14,0},{1,15},{3,5}... | collective-permute-start | bytes 491528 | tf_op jit(solution)/shard_map/ppermute | solution.py:38
  25.4 8.8 %collective-permute-start.18 = (bf16[160,512]{1,0:T(8,128)(2,1)S(1)}, bf16[160,512]{1,0:T(8,128)(2,1)S(1)}, u32[]{:S(2)}, u32[]{:S(2)}) collective-permute-start(bf16[160,512]{1,0:T(8,128)(2,1)S(1)} %pad_maximum_fusion.1), channel_id=1, source_target_pairs={{0,2},{2,0},{4,6},{6,4},{8,10},{10,8},{12,14},{14,12},{1,3},{3,1},... | collective-permute-start | bytes 491528 | tf_op jit(solution)/shard_map/ppermute | solution.py:38
  31.0 7.2 %collective-permute-start.15 = (bf16[160,512]{1,0:T(8,128)(2,1)S(1)}, bf16[160,512]{1,0:T(8,128)(2,1)S(1)}, u32[]{:S(2)}, u32[]{:S(2)}) collective-permute-start(bf16[160,512]{1,0:T(8,128)(2,1)S(1)} %collective-permute-done.14), channel_id=1, source_target_pairs={{0,2},{2,0},{4,6},{6,4},{8,10},{10,8},{12,14},{14,12},{1,3},{3,1},... | collective-permute-start | bytes 491528 | tf_op jit(solution)/shard_map/ppermute | solution.py:39
  34.2 9.3 %collective-permute-start.19 = (bf16[160,512]{1,0:T(8,128)(2,1)S(1)}, bf16[160,512]{1,0:T(8,128)(2,1)S(1)}, u32[]{:S(2)}, u32[]{:S(2)}) collective-permute-start(bf16[160,512]{1,0:T(8,128)(2,1)S(1)} %collective-permute-done.18), channel_id=1, source_target_pairs={{0,14},{2,4},{4,2},{6,8},{8,6},{10,12},{12,10},{14,0},{1,15},{3,5}... | collective-permute-start | bytes 491528 | tf_op jit(solution)/shard_map/ppermute | solution.py:39
  38.2 8.4 %collective-permute-start.16 = (bf16[160,512]{1,0:T(8,128)(2,1)S(1)}, bf16[160,512]{1,0:T(8,128)(2,1)S(1)}, u32[]{:S(2)}, u32[]{:S(2)}) collective-permute-start(bf16[160,512]{1,0:T(8,128)(2,1)S(1)} %collective-permute-done.15), channel_id=1, source_target_pairs={{0,14},{2,4},{4,2},{6,8},{8,6},{10,12},{12,10},{14,0},{1,15},{3,5}... | collective-permute-start | bytes 491528 | tf_op jit(solution)/shard_map/ppermute | solution.py:40
  43.6 7.2 %collective-permute-start.20 = (bf16[160,512]{1,0:T(8,128)(2,1)S(1)}, bf16[160,512]{1,0:T(8,128)(2,1)S(1)}, u32[]{:S(2)}, u32[]{:S(2)}) collective-permute-start(bf16[160,512]{1,0:T(8,128)(2,1)S(1)} %collective-permute-done.19), channel_id=1, source_target_pairs={{0,2},{2,0},{4,6},{6,4},{8,10},{10,8},{12,14},{14,12},{1,3},{3,1},... | collective-permute-start | bytes 491528 | tf_op jit(solution)/shard_map/ppermute | solution.py:40
  50.8 1.1 %copy-start.1 = (f32[1,320,512]{2,1,0:T(8,128)S(1)}, f32[1,320,512]{2,1,0:T(8,128)}, u32[]{:S(2)}) copy-start(f32[1,320,512]{2,1,0:T(8,128)} %param.11) | copy-start | bytes 1966084
  52.1 8.5 %collective-permute-start.9 = (bf16[160,512]{1,0:T(8,128)(2,1)S(1)}, bf16[160,512]{1,0:T(8,128)(2,1)S(1)}, u32[]{:S(2)}, u32[]{:S(2)}) collective-permute-start(bf16[160,512]{1,0:T(8,128)(2,1)S(1)} %select_convert_fusion.3), channel_id=1, source_target_pairs={{0,128},{128,0},{1,129},{129,1},{2,130},{130,2},{3,131},{131,3},{4... | collective-permute-start | bytes 491528 | tf_op jit(solution)/shard_map/cond/branch_3_fun/ppermute | solution.py:14
  60.6 20.1 %collective-permute-start.10 = (bf16[160,512]{1,0:T(8,128)(2,1)S(1)}, bf16[160,512]{1,0:T(8,128)(2,1)S(1)}, u32[]{:S(2)}, u32[]{:S(2)}) collective-permute-start(bf16[160,512]{1,0:T(8,128)(2,1)S(1)} %convert_element_type.146), channel_id=1, source_target_pairs={{0,512},{512,0},{1,513},{513,1},{2,514},{514,2},{3,515},{515,3},{4... | collective-permute-start | bytes 491528 | tf_op jit(solution)/shard_map/cond/branch_3_fun/ppermute | solution.py:14
  80.8 7.2 %collective-permute-start.11 = (bf16[160,512]{1,0:T(8,128)(2,1)S(1)}, bf16[160,512]{1,0:T(8,128)(2,1)S(1)}, u32[]{:S(2)}, u32[]{:S(2)}) collective-permute-start(bf16[160,512]{1,0:T(8,128)(2,1)S(1)} %get-tuple-element.104), channel_id=1, source_target_pairs={{0,128},{128,0},{1,129},{129,1},{2,130},{130,2},{3,131},{131,3},{4... | collective-permute-start | bytes 491528 | tf_op jit(solution)/shard_map/cond/branch_3_fun/ppermute | solution.py:14
  89.1 0.7 copy-start.2
